TPU v7x, 32 devices: a whole 2x2x4 slice. The times are simulated.
32 devices in a mesh: dp: 4 (over z), proto: 8 (over y, x, core).
Axes of the slice: x: 2, y: 2, z: 4, core: 2. Of those that a mesh axis runs over, the one named last changes fastest.
Arguments:
- teacher_rows: bfloat16 [1024, 256], P(('dp', 'proto')), may hold values from -48 to 48
- student_rows: bfloat16 [1024, 256], P(('dp', 'proto')), may hold values from -48 to 48
- teacher_protos: bfloat16 [65536, 256], P('proto'), may hold values from -48 to 48
- student_protos: bfloat16 [65536, 256], P('proto'), may hold values from -48 to 48
Outputs:
- row_grads: float32 [1024, 256], P(('dp', 'proto'))
- proto_grads: float32 [65536, 256], P('proto')
All inputs are finite; a program needn't handle non-finite values.
Results may differ from a plain program's by a relative error of at most 0.0034.
Values may be sent and summed in bfloat16 or wider, within the bound.
A program may use at most 128 MiB of HBM per device.

v0:
```python
import jax
import jax.numpy as jnp
from jax import lax
from jax.sharding import PartitionSpec as P

ITERS = 3


teacher_temp = 0.04
student_temp = 0.1
norm_eps = 1e-06


def unit_rows(values):
    vf = values.astype(jnp.float32)
    length = jnp.sqrt(jnp.sum(vf * vf, axis=-1, keepdims=True) + norm_eps)
    return (vf / length, length)


def project_out(grads, unit, length):
    return (grads - jnp.sum(grads * unit, axis=1, keepdims=True) * unit) / length


def body(teacher_rows, student_rows, teacher_protos, student_protos):
    whole_t, whole_s = (
        lax.all_gather(teacher_rows, "proto", axis=0, tiled=True),
        lax.all_gather(student_rows, "proto", axis=0, tiled=True),
    )
    n_rows = whole_t.shape[0] * lax.axis_size("dp")
    n_protos = teacher_protos.shape[0] * lax.axis_size("proto")
    t_unit = unit_rows(whole_t)[0].astype(jnp.bfloat16)
    s_unit = unit_rows(whole_s)[0].astype(jnp.bfloat16)
    wt_unit = unit_rows(teacher_protos)[0].astype(jnp.bfloat16)
    ws_full, ws_length = unit_rows(student_protos)
    ws_unit = ws_full.astype(jnp.bfloat16)
    teach_exp = jnp.exp(
        jnp.einsum("rd,kd->rk", t_unit, wt_unit, preferred_element_type=jnp.float32) / teacher_temp
    )
    student_exp = jnp.exp(
        jnp.einsum("rd,kd->rk", s_unit, ws_unit, preferred_element_type=jnp.float32) / student_temp
    )
    student_part = jnp.sum(student_exp, axis=1)
    row_weight = jnp.ones((whole_t.shape[0],), jnp.float32)
    col_weight = None
    total = None
    for step in range(ITERS):
        col_part = jnp.dot(row_weight, teach_exp, precision=lax.Precision.HIGHEST)
        col_weight = 1.0 / (n_protos * lax.psum(col_part, "dp"))
        row_part = jnp.dot(teach_exp, col_weight, precision=lax.Precision.HIGHEST)
        row_sum = lax.psum(row_part, "proto")
        row_weight = 1.0 / (n_rows * row_sum)
    total = lax.psum(student_part, "proto")
    targets = n_rows * teach_exp * row_weight[:, None] * col_weight[None, :]
    probs = student_exp / total[:, None]
    grad_z = ((probs - targets) / student_temp).astype(jnp.bfloat16)
    g_rows = lax.psum_scatter(
        jnp.einsum("rk,kd->rd", grad_z, ws_unit, preferred_element_type=jnp.float32),
        "proto",
        scatter_dimension=0,
        tiled=True,
    )
    own_unit, own_length = unit_rows(student_rows)
    row_grads = project_out(g_rows, own_unit, own_length)
    partial_protos = jnp.einsum("rk,rd->kd", grad_z, s_unit, preferred_element_type=jnp.float32)
    factor = n_protos / n_rows
    g_protos = lax.psum(partial_protos, "dp")
    proto_grads = factor * project_out(g_protos, ws_full, ws_length)
    return (row_grads, proto_grads)


def solution(mesh):
    placed = (
        P(("dp", "proto"), None),
        P(("dp", "proto"), None),
        P("proto", None),
        P("proto", None),
    )
    return jax.shard_map(
        body,
        mesh=mesh,
        in_specs=placed,
        out_specs=(P(("dp", "proto"), None), P("proto", None)),
        check_vma=False,
    )
```

profile of v0, /device:TPU:0, one launch (start us, length us, event | category | flops | bytes accessed | tf_op | source)
XLA Modules:
  0.0 508.4 jit_solution(12256862403181698168)
XLA Ops:
  8.0 0.0 reduce-scatter.2.cloned.1.call-start
  8.0 10.8 %all_gather.7 = bf16[256,256]{1,0:T(8,128)(2,1)S(1)} all-gather(bf16[32,256]{1,0:T(8,128)(2,1)} %param.4), channel_id=1, replica_groups=mesh['dp'=4,'proto'=8] {'proto'}, dimensions={0}, use_global_device_ids=true | all-gather | bytes 147456 | tf_op jit(solution)/shard_map/all_gather | solution.py:26
  18.9 0.1 fusion.12
  19.0 3.3 fusion.3
  22.4 4.1 fusion
  26.5 0.0 copy-start
  26.5 3.4 copy-done
  29.9 4.0 fusion.17
  33.9 19.3 %psum.57 = f32[8192]{0:T(1024)S(1)} all-reduce(f32[8192]{0:T(1024)S(1)} %bitcast.29), channel_id=1, replica_groups=mesh['dp'=4,'proto'=8] {'dp'}, use_global_device_ids=true, to_apply=%region_6.0 | all-reduce | flops 8192 | bytes 65536 | tf_op jit(solution)/shard_map/psum | solution.py:48
  53.2 8.9 %fusion.24 = f32[1,256]{1,0:T(1,128)S(1)} fusion(f32[256,8192]{1,0:T(8,128)} %copy-done, f32[8192,1]{0,1:T(1,128)S(1)} %bitcast.25), kind=kOutput, calls=%fused_computation.48 | convolution fusion | flops 25165824 | bytes 8422400 | tf_op jit(solution)/shard_map/dot_general | solution.py:49
  62.1 12.0 %psum.58 = f32[256]{0:T(256)S(1)} all-reduce(f32[256]{0:T(256)S(1)} %bitcast.31), channel_id=1, replica_groups=mesh['dp'=4,'proto'=8] {'proto'}, use_global_device_ids=true, to_apply=%region_7.0 | all-reduce | flops 256 | bytes 2048 | tf_op jit(solution)/shard_map/psum | solution.py:50
  74.1 7.4 %fusion.25 = f32[1,8192]{1,0:T(1,128)S(1)} fusion(f32[256,1]{0,1:T(1,128)S(1)} %bitcast.32, f32[256,8192]{1,0:T(8,128)} %copy-done), kind=kOutput, calls=%fused_computation.49 | convolution fusion | flops 25165824 | bytes 8422400 | tf_op jit(solution)/shard_map/dot_general | solution.py:47
  81.5 15.8 %psum.59 = f32[8192]{0:T(1024)S(1)} all-reduce(f32[8192]{0:T(1024)S(1)} %bitcast.26), channel_id=1, replica_groups=mesh['dp'=4,'proto'=8] {'dp'}, use_global_device_ids=true, to_apply=%region_8.0 | all-reduce | flops 8192 | bytes 65536 | tf_op jit(solution)/shard_map/psum | solution.py:48
  97.3 8.9 %fusion.26 = f32[1,256]{1,0:T(1,128)S(1)} fusion(f32[256,8192]{1,0:T(8,128)} %copy-done, f32[8192,1]{0,1:T(1,128)S(1)} %bitcast.27), kind=kOutput, calls=%fused_computation.50 | convolution fusion | flops 25165824 | bytes 8422400 | tf_op jit(solution)/shard_map/dot_general | solution.py:49
  106.2 11.8 %psum.60 = f32[256]{0:T(256)S(1)} all-reduce(f32[256]{0:T(256)S(1)} %bitcast.33), channel_id=1, replica_groups=mesh['dp'=4,'proto'=8] {'proto'}, use_global_device_ids=true, to_apply=%region_9.0 | all-reduce | flops 256 | bytes 2048 | tf_op jit(solution)/shard_map/psum | solution.py:50
  118.0 0.0 copy-start.6
  118.0 7.4 %fusion.27 = f32[1,8192]{1,0:T(1,128)S(1)} fusion(f32[256,1]{0,1:T(1,128)S(1)} %bitcast.34, f32[256,8192]{1,0:T(8,128)} %copy-done), kind=kOutput, calls=%fused_computation.51 | convolution fusion | flops 25165824 | bytes 8422400 | tf_op jit(solution)/shard_map/dot_general | solution.py:47
  125.4 17.5 %psum.61 = f32[8192]{0:T(1024)S(1)} all-reduce(f32[8192]{0:T(1024)S(1)} %bitcast.28), channel_id=1, replica_groups=mesh['dp'=4,'proto'=8] {'dp'}, use_global_device_ids=true, to_apply=%region_10.0 | all-reduce | flops 8192 | bytes 65536 | tf_op jit(solution)/shard_map/psum | solution.py:48
  142.9 0.0 copy-start.1
  143.0 9.0 %fusion.28 = f32[1,256]{1,0:T(1,128)S(1)} fusion(f32[256,8192]{1,0:T(8,128)} %copy-done, f32[8192,1]{0,1:T(1,128)S(1)} %bitcast.24), kind=kOutput, calls=%fused_computation.52 | convolution fusion | flops 25165824 | bytes 8422400 | tf_op jit(solution)/shard_map/dot_general | solution.py:49
  152.0 0.0 copy-done.6
  152.0 9.0 %all_gather.6 = bf16[256,256]{1,0:T(8,128)(2,1)S(1)} all-gather(bf16[32,256]{1,0:T(8,128)(2,1)S(1)} %copy-done.6), channel_id=1, replica_groups=mesh['dp'=4,'proto'=8] {'proto'}, dimensions={0}, use_global_device_ids=true | all-gather | bytes 147456 | tf_op jit(solution)/shard_map/all_gather | solution.py:27
  161.1 0.1 fusion.10
  161.2 0.0 copy-done.1
  161.2 1.2 fusion.2
  162.4 4.8 fusion.23
  167.2 13.2 %all-reduce = (f32[256]{0:T(256)S(1)}, f32[256]{0:T(256)S(1)}) all-reduce(f32[256]{0:T(256)S(1)} %bitcast.30, f32[256]{0:T(256)S(1)} %get-tuple-element.4), channel_id=1, replica_groups=mesh['dp'=4,'proto'=8] {'proto'}, use_global_device_ids=true, to_apply=%region_11.0 | all-reduce | flops 512 | bytes 4096 | tf_op jit(solution)/shard_map/psum | solution.py:50
  180.4 0.0 copy-start.2
  180.4 7.0 %multiply_convert_fusion = bf16[256,8192]{1,0:T(8,128)(2,1)S(1)} fusion(f32[256,8192]{1,0:T(8,128)} %copy-done, f32[256,8192]{1,0:T(8,128)} %get-tuple-element.5, f32[8192]{0:T(1024)S(1)} %multiply_divide_fusion, f32[256]{0:T(256)S(1)} %divide_multiply_fusion.1, f32[256]{0:T(256)S(1)} %get-tuple-element.3), kind=kLoop, calls=%fused_computation.13 | loop fusion | flops 12582912 | bytes 21006336 | tf_op jit(solution)/shard_map/convert_element_type | solution.py:55
  187.4 0.0 copy-start.5
  187.4 1.9 copy-done.5
  189.3 0.0 copy-done.2
  189.3 2.1 fusion.7
  191.4 0.0 reduce-scatter.2.cloned.1.call-update
  191.5 0.0 all-reduce.3.cloned.1.call-start
  191.5 7.0 %fusion.20 = f32[8192,256]{1,0:T(8,128)} fusion(bf16[256,8192]{1,0:T(8,128)(2,1)} %copy-done.5, bf16[256,256]{1,0:T(8,128)(2,1)S(1)} %all_gather.6, f32[256]{0:T(256)S(1)} %add_sqrt_fusion.3), kind=kOutput, calls=%fused_computation.46 | convolution fusion | flops 1073938432 | bytes 12715008 | tf_op jit(solution)/shard_map/rk,rd->kd/dot_general | solution.py:64
  198.5 0.0 all-reduce.3.cloned.1.call-update
  198.5 0.1 fusion.16
  198.6 23.1 %reduce-scatter.2.cloned.1.call-done = f32[32,256]{1,0:T(8,128)} async-done(((f32[256,256]{1,0:T(8,128)}), f32[32,256]{1,0:T(8,128)}) %reduce-scatter.2.cloned.1.call-update) | async-done | bytes 32784 | tf_op jit(solution)/shard_map/reduce_scatter | solution.py:56
  221.7 0.9 multiply_reduce_fusion.1
  222.7 1.5 subtract_divide_fusion
  224.1 261.6 %all-reduce.3.cloned.1.call-done = f32[8192,256]{1,0:T(8,128)} async-done(((f32[8192,256]{1,0:T(8,128)}), f32[8192,256]{1,0:T(8,128)}) %all-reduce.3.cloned.1.call-update) | async-done | bytes 8388624 | tf_op jit(solution)/shard_map/psum | solution.py:66
  485.7 0.0 copy-start.3
  485.7 0.0 copy-start.4
  485.7 6.7 %multiply_reduce_fusion = f32[8192]{0:T(1024)S(1)} fusion(f32[8192,256]{1,0:T(8,128)} %all-reduce.3.cloned.1.call-done, f32[8192]{0:T(1024)S(1)} %add_sqrt_fusion.1, bf16[8192,256]{1,0:T(8,128)(2,1)} %param.7), kind=kLoop, calls=%fused_computation.12 | loop fusion | flops 8380416 | bytes 12648448 | tf_op jit(solution)/shard_map/reduce_sum | solution.py:21
  492.4 0.0 copy-done.3
  492.4 1.6 copy-done.4
  494.0 6.9 %divide_multiply_fusion = f32[8192,256]{1,0:T(8,128)} fusion(f32[8192,256]{1,0:T(8,128)S(1)} %copy-done.4, f32[8192]{0:T(1024)S(1)} %multiply_reduce_fusion, f32[8192]{0:T(1024)S(1)} %add_sqrt_fusion.1, bf16[8192,256]{1,0:T(8,128)(2,1)S(1)} %copy-done.3), kind=kLoop, calls=%fused_computation.11 | loop fusion | flops 12582912 | bytes 21037056 | tf_op jit(solution)/shard_map/mul | solution.py:67
  (11 shorter events, 0.1 us)
Async XLA Ops:
  8.0 213.7 %reduce-scatter.2.cloned.1.call-start = ((), (), s32[]{:S(2)}) async-start(), calls=%async_computation.1 | async-start | bytes 294912 | tf_op jit(solution)/shard_map/reduce_scatter | solution.py:56
  26.5 3.4 copy-start
  118.0 34.1 %copy-start.6 = (bf16[32,256]{1,0:T(8,128)(2,1)S(1)}, bf16[32,256]{1,0:T(8,128)(2,1)}, u32[]{:S(2)}) copy-start(bf16[32,256]{1,0:T(8,128)(2,1)} %param.5) | copy-start | bytes 49156
  142.9 18.3 %copy-start.1 = (bf16[8192,256]{1,0:T(8,128)(2,1)S(1)}, bf16[8192,256]{1,0:T(8,128)(2,1)}, u32[]{:S(2)}) copy-start(bf16[8192,256]{1,0:T(8,128)(2,1)} %param.7) | copy-start | bytes 12582916
  180.4 8.9 %copy-start.2 = (bf16[8192,256]{1,0:T(8,128)(2,1)S(1)}, bf16[8192,256]{1,0:T(8,128)(2,1)}, u32[]{:S(2)}) copy-start(bf16[8192,256]{1,0:T(8,128)(2,1)} %param.7) | copy-start | bytes 12582916
  187.4 1.9 copy-start.5
  191.5 294.2 %all-reduce.3.cloned.1.call-start = ((), (), s32[]{:S(2)}) async-start(), calls=%async_computation.2 | async-start | bytes 16777216 | tf_op jit(solution)/shard_map/psum | solution.py:66
  485.7 6.7 %copy-start.3 = (bf16[8192,256]{1,0:T(8,128)(2,1)S(1)}, bf16[8192,256]{1,0:T(8,128)(2,1)}, u32[]{:S(2)}) copy-start(bf16[8192,256]{1,0:T(8,128)(2,1)} %param.7) | copy-start | bytes 12582916
  485.7 8.3 %copy-start.4 = (f32[8192,256]{1,0:T(8,128)S(1)}, f32[8192,256]{1,0:T(8,128)}, u32[]{:S(2)}) copy-start(f32[8192,256]{1,0:T(8,128)} %all-reduce.3.cloned.1.call-done) | copy-start | bytes 25165828
Sparse Core Ops, SparseCore 0:
  191.6 30.1 reduce-scatter.1
Sparse Core Ops, SparseCore 1:
  198.6 287.1 all-reduce.2
where the time goes:
time: 509 us; the launch traced here: 508 us
  waiting for transfers between devices  285 us (56%)
  blocking collectives  109 us (21%)
  matrix products  63.7 us (13%)
  other arithmetic  28 us (6%)
  between operations  15.7 us (3%)
  local copies, waits for them, and re-layouts  6.91 us (1%)
    psum x1, waiting for transfers between devices, body(): g_protos = lax.psum(partial_protos, 'dp')  262 us
    psum x3, blocking collectives, body(): col_weight = 1.0 / (n_protos * lax.psum(col_part, 'dp'))  52.5 us
    psum x3, blocking collectives, body(): row_sum = lax.psum(row_part, 'proto')  36.9 us
    dot_general x3, matrix products, body(): row_part = jnp.dot(teach_exp, col_weight, precision=lax.Precision.HIGHEST)  26.8 us
    reduce_scatter x1, waiting for transfers between devices, body(): lax.psum_scatter(jnp.einsum('rk,kd->rd', grad_z, ws_unit, preferred_eleme...  23.1 us
    dot_general x3, matrix products, body(): col_part = jnp.dot(row_weight, teach_exp, precision=lax.Precision.HIGHEST)  18.9 us
    all_gather x1, blocking collectives, body(): lax.all_gather(teacher_rows, 'proto', axis=0, tiled=True)  10.8 us
  transfers between devices with their start and end apart: 2, of which 2 were waited for; matrix products, arithmetic and copies ran while one was open for 2% of the time, Pallas kernels for 0%

commit v1 on v0

v1 whole, which is shorter than its diff:
```python
import functools
import math

import jax
import jax.numpy as jnp
from jax import lax
from jax.experimental import pallas as pl
from jax.experimental.pallas import tpu as pltpu
from jax.sharding import PartitionSpec as P

ITERS = 3
LANES = 128

teacher_temp = 0.04
student_temp = 0.1
norm_eps = 1e-06
LOG2E = math.log2(math.e)
VMEM_BYTES = 56 * 1024 * 1024

MESH = pl.DeviceIdType.MESH
f32 = jnp.float32
bf16 = jnp.bfloat16


def inv_norm(vf):
    return lax.rsqrt(jnp.sum(vf * vf, axis=-1, keepdims=True) + norm_eps)


def unit_bf16(values):
    vf = values.astype(f32)
    return (vf * inv_norm(vf)).astype(bf16)


def dot_nn(a, b):
    return jnp.dot(a, b, preferred_element_type=f32)


def fold8(x):
    return jnp.sum(x.reshape(x.shape[0] // 8, 8, x.shape[1]), axis=0)


def greet(n_dp, n_proto):
    me_d, me_p = lax.axis_index("dp"), lax.axis_index("proto")
    barrier = pltpu.get_barrier_semaphore()
    for k in range(1, n_dp):
        pl.semaphore_signal(barrier, inc=1, device_id={"dp": lax.rem(me_d + k, n_dp)}, device_id_type=MESH)
    for k in range(1, n_proto):
        pl.semaphore_signal(barrier, inc=1, device_id={"proto": lax.rem(me_p + k, n_proto)}, device_id_type=MESH)
    return barrier


def sinkhorn_kernel(
    n_dp, n_proto, n_protos, tile, small,
    tT_ref, sT_ref, wt_hbm, ws_hbm, out_ref,
    e_ref, wt_ref, ws_ref, rxd, rxp, in_sem, sd, rd, sp, rp,
):
    n_rows = tT_ref.shape[1]
    own = wt_ref.shape[0]
    rb = n_rows // LANES
    me_d, me_p = lax.axis_index("dp"), lax.axis_index("proto")
    off = pl.multiple_of(me_d * own, own)
    in_t = pltpu.make_async_copy(wt_hbm.at[pl.ds(off, own)], wt_ref, in_sem.at[0])
    in_s = pltpu.make_async_copy(ws_hbm.at[pl.ds(off, own)], ws_ref, in_sem.at[1])
    in_t.start()
    in_s.start()
    barrier = greet(n_dp, n_proto)
    in_t.wait()

    zero = jnp.zeros((8, n_rows), f32)

    def first(i, acc):
        at = pl.ds(pl.multiple_of(i * tile, tile), tile)
        z = dot_nn(unit_bf16(wt_ref[at, :]), tT_ref[...])
        e = jnp.exp2(z * (LOG2E / teacher_temp))
        e_ref[at, :] = e
        col = 1.0 / (n_protos * jnp.sum(e, axis=1, keepdims=True))
        return acc + fold8(e * col)

    def student(i, acc):
        at = pl.ds(pl.multiple_of(i * tile, tile), tile)
        z = dot_nn(unit_bf16(ws_ref[at, :]), sT_ref[...])
        return acc + fold8(jnp.exp2(z * (LOG2E / student_temp)))

    def put(it, acc, part):
        row = jnp.sum(acc, axis=0, keepdims=True)
        for k in range(rb):
            rxd[it, me_d, part * rb + k : part * rb + k + 1, :] = row[:, k * LANES : (k + 1) * LANES]

    def take(tot, part):
        return jnp.concatenate([tot[part * rb + k : part * rb + k + 1, :] for k in range(rb)], axis=1)

    def sends(it, ref, me, n, axis, send, recv):
        copies = []
        for k in range(1, n):
            copies.append(
                pltpu.make_async_remote_copy(
                    src_ref=ref.at[it, me],
                    dst_ref=ref.at[it, me],
                    send_sem=send.at[it, k],
                    recv_sem=recv.at[it, k],
                    device_id={axis: lax.rem(me + k, n)},
                    device_id_type=MESH,
                )
            )
        for c in copies:
            c.start()
        return copies

    acc = lax.fori_loop(0, own // tile, first, zero)
    row_weight = jnp.ones((1, n_rows), f32)
    total = None
    acc_s = zero
    in_s.wait()
    for it in range(ITERS):
        prev = row_weight
        if it > 0:

            def again(i, acc, prev=prev):
                at = pl.ds(pl.multiple_of(i * small, small), small)
                e = e_ref[at, :]
                col = 1.0 / (n_protos * jnp.sum(e * prev, axis=1, keepdims=True))
                return acc + fold8(e * col)

            acc = lax.fori_loop(0, own // small, again, zero)
        put(it, acc, 0)
        put(it, acc_s, 1)
        if it == 0:
            pl.semaphore_wait(barrier, n_dp + n_proto - 2)
        copies = sends(it, rxd, me_d, n_dp, "dp", sd, rd)
        if it == 0:
            acc_s = lax.fori_loop(0, own // tile, student, zero)
        for c in copies:
            c.wait()
        part = rxd[it, 0]
        for k in range(1, n_dp):
            part = part + rxd[it, k]
        rxp[it, me_p] = part
        copies = sends(it, rxp, me_p, n_proto, "proto", sp, rp)
        for c in copies:
            c.wait()
        tot = rxp[it, 0]
        for k in range(1, n_proto):
            tot = tot + rxp[it, k]
        row_weight = 1.0 / (n_rows * take(tot, 0))
        total = take(tot, 1)
    out_ref[...] = jnp.zeros_like(out_ref)
    out_ref[0:1, :] = prev
    out_ref[1:2, :] = row_weight * (n_rows / student_temp)
    out_ref[2:3, :] = (1.0 / student_temp) / total


def sinkhorn(tT, sT, wt, ws, n_dp, n_proto):
    d, n_rows = tT.shape
    own = wt.shape[0] // n_dp
    rb = n_rows // LANES
    sems = pltpu.SemaphoreType.DMA
    vm = pl.BlockSpec(memory_space=pltpu.VMEM)
    anym = pl.BlockSpec(memory_space=pl.ANY)
    return pl.pallas_call(
        functools.partial(sinkhorn_kernel, n_dp, n_proto, wt.shape[0] * n_proto, 256, 32),
        out_shape=jax.ShapeDtypeStruct((8, n_rows), f32),
        in_specs=[vm, vm, anym, anym],
        out_specs=vm,
        scratch_shapes=[
            pltpu.VMEM((own, n_rows), f32),
            pltpu.VMEM((own, d), bf16),
            pltpu.VMEM((own, d), bf16),
            pltpu.VMEM((ITERS, n_dp, 2 * rb, LANES), f32),
            pltpu.VMEM((ITERS, n_proto, 2 * rb, LANES), f32),
            sems((2,)),
            sems((ITERS, n_dp)),
            sems((ITERS, n_dp)),
            sems((ITERS, n_proto)),
            sems((ITERS, n_proto)),
        ],
        compiler_params=pltpu.CompilerParams(collective_id=0, has_side_effects=True, vmem_limit_bytes=VMEM_BYTES),
        name="sinkhorn",
    )(tT, sT, wt, ws)


def backward_kernel(
    n_dp, n_protos, tT_ref, sT_ref, s_ref, rows_ref, wt_ref, ws_ref, out_ref, grow_ref, dz_ref
):
    n_rows = tT_ref.shape[1]
    mine = n_rows // n_dp
    a_prev, a_last, p_last = rows_ref[0:1, :], rows_ref[1:2, :], rows_ref[2:3, :]
    zt = dot_nn(unit_bf16(wt_ref[...]), tT_ref[...])
    wsf = ws_ref[...].astype(f32)
    ws_inv = inv_norm(wsf)
    ws_unit = wsf * ws_inv
    ws_half = ws_unit.astype(bf16)
    zs = dot_nn(ws_half, sT_ref[...])
    e = jnp.exp2(zt * (LOG2E / teacher_temp))
    col = 1.0 / (n_protos * jnp.sum(e * a_prev, axis=1, keepdims=True))
    probs = jnp.exp2(zs * (LOG2E / student_temp)) * p_last
    dz = (probs - (e * a_last) * col).astype(bf16)
    dz_ref[...] = dz
    g = dot_nn(dz, s_ref[...])
    factor = n_protos / n_rows
    proj = jnp.sum(g * ws_unit, axis=1, keepdims=True)
    out_ref[...] = (g - proj * ws_unit) * (factor * ws_inv)
    at = pl.multiple_of(lax.axis_index("dp") * mine, mine)
    part = lax.dot_general(
        dz_ref[:, pl.ds(at, mine)], ws_half, (((0,), (0,)), ((), ())), preferred_element_type=f32
    )

    @pl.when(pl.program_id(0) == 0)
    def _():
        grow_ref[...] = jnp.zeros_like(grow_ref)

    grow_ref[...] += part


def backward(tT, sT, s, rows, wt, ws, n_dp, n_proto, tile=256):
    d, n_rows = tT.shape
    n_own = wt.shape[0]
    const = lambda shape: pl.BlockSpec(shape, lambda i: (0, 0))
    tiled = pl.BlockSpec((tile, d), lambda i: (i, 0))
    mine = n_rows // n_dp
    return pl.pallas_call(
        functools.partial(backward_kernel, n_dp, n_own * n_proto),
        grid=(n_own // tile,),
        out_shape=(jax.ShapeDtypeStruct((n_own, d), f32), jax.ShapeDtypeStruct((mine, d), f32)),
        in_specs=[const((d, n_rows)), const((d, n_rows)), const((n_rows, d)), const((8, n_rows)), tiled, tiled],
        out_specs=(tiled, const((mine, d))),
        scratch_shapes=[pltpu.VMEM((tile, n_rows), bf16)],
        compiler_params=pltpu.CompilerParams(vmem_limit_bytes=VMEM_BYTES),
        name="backward",
    )(tT, sT, s, rows, wt, ws)


def scatter_kernel(n, g_ref, s_ref, out_ref, rx, send, recv):
    me = lax.axis_index("proto")
    own = out_ref.shape[0]
    barrier = pltpu.get_barrier_semaphore()
    for k in range(1, n):
        pl.semaphore_signal(barrier, inc=1, device_id={"proto": lax.rem(me + k, n)}, device_id_type=MESH)
    pl.semaphore_wait(barrier, n - 1)
    copies = []
    for k in range(1, n):
        to = lax.rem(me + k, n)
        copies.append(
            pltpu.make_async_remote_copy(
                src_ref=g_ref.at[pl.ds(pl.multiple_of(to * own, own), own)],
                dst_ref=rx.at[me],
                send_sem=send.at[k],
                recv_sem=recv.at[k],
                device_id={"proto": to},
                device_id_type=MESH,
            )
        )
    for c in copies:
        c.start()
    rx[me] = g_ref[pl.ds(pl.multiple_of(me * own, own), own), :]
    sf = s_ref[...].astype(f32)
    inv = inv_norm(sf)
    unit = sf * inv
    for c in copies:
        c.wait()
    g = rx[0]
    for k in range(1, n):
        g = g + rx[k]
    out_ref[...] = (g - jnp.sum(g * unit, axis=1, keepdims=True) * unit) * inv


def scatter_rows(grow, student_rows, n_proto):
    vm = pl.BlockSpec(memory_space=pltpu.VMEM)
    own, d = student_rows.shape
    return pl.pallas_call(
        functools.partial(scatter_kernel, n_proto),
        out_shape=jax.ShapeDtypeStruct((own, d), f32),
        in_specs=[vm, vm],
        out_specs=vm,
        scratch_shapes=[
            pltpu.VMEM((n_proto, own, d), f32),
            pltpu.SemaphoreType.DMA((n_proto,)),
            pltpu.SemaphoreType.DMA((n_proto,)),
        ],
        compiler_params=pltpu.CompilerParams(collective_id=1, has_side_effects=True),
        name="scatter_rows",
    )(grow, student_rows)


def body(teacher_rows, student_rows, teacher_protos, student_protos):
    n_dp, n_proto = lax.axis_size("dp"), lax.axis_size("proto")
    d = teacher_rows.shape[1]
    both = jnp.concatenate([unit_bf16(teacher_rows), unit_bf16(student_rows)], axis=1)
    both = lax.all_gather(both, ("dp", "proto"), axis=0, tiled=True)
    s_unit = both[:, d:]
    tT, sT = both[:, :d].T, s_unit.T
    rows = sinkhorn(tT, sT, teacher_protos, student_protos, n_dp, n_proto)
    proto_grads, grow = backward(tT, sT, s_unit, rows, teacher_protos, student_protos, n_dp, n_proto)
    row_grads = scatter_rows(grow, student_rows, n_proto)
    return (row_grads, proto_grads)


def solution(mesh):
    rows = P(("dp", "proto"), None)
    protos = P("proto", None)
    return jax.shard_map(
        body,
        mesh=mesh,
        in_specs=(rows, rows, protos, protos),
        out_specs=(rows, protos),
        check_vma=False,
    )
```

time: 509 us -> 168 us (0.33)
  waiting for transfers between devices: 285 us -> 57.5 us
  blocking collectives: 109 us -> 0 us
  Pallas kernels: 0 us -> 87.6 us
  matrix products: 63.7 us -> 0 us
  other arithmetic: 28 us -> 3.12 us
    psum x1 -> x0, waiting for transfers between devices: 262 us -> none  [body(): g_protos = lax.psum(partial_protos, 'dp')]
    psum x6 -> x0, blocking collectives: 89.5 us -> none  [the longest x3 52.5 us: body(): col_weight = 1.0 / (n_protos * lax.psum(col_part, 'dp'))]
    pallas_call x0 -> x3, Pallas kernels: none -> 87.6 us  [the longest x1 41.5 us: sinkhorn(): pl.pallas_call(functools.partial(sinkhorn_kernel, n_dp, n_proto, wt.shape...]
    dot_general x10 -> x0, matrix products: 63.7 us -> none  [the longest x3 26.8 us: body(): row_part = jnp.dot(teach_exp, col_weight, precision=lax.Precision.HIGHEST)]
    all_gather x0 -> x1, waiting for transfers between devices: none -> 57.5 us  [body(): both = lax.all_gather(both, ('dp', 'proto'), axis=0, tiled=True)]
    reduce_scatter x1 -> x0, waiting for transfers between devices: 23.1 us -> none  [body(): lax.psum_scatter(jnp.einsum('rk,kd->rd', grad_z, ws_unit, preferred_eleme...]
    all_gather x2 -> x0, blocking collectives: 19.9 us -> none  [the longest x1 10.8 us: body(): lax.all_gather(teacher_rows, 'proto', axis=0, tiled=True)]
    reduce_sum x7 -> x2, other arithmetic: 12.5 us -> 1.67 us  [inv_norm(): return lax.rsqrt(jnp.sum(vf * vf, axis=-1, keepdims=True) + norm_eps)]
  transfers between devices with their start and end apart: 2 -> 1, of which waited for: 2 -> 1; matrix products, arithmetic and copies ran while one was open for 2% -> 0% of each run, Pallas kernels for 0% -> 0%
where the time goes in v1:
time: 168 us
  Pallas kernels  87.6 us (52%)
  waiting for transfers between devices  57.5 us (34%)
  between operations  14.1 us (8%)
  local copies, waits for them, and re-layouts  5.5 us (3%)
  other arithmetic  3.12 us (2%)
    all_gather x1, waiting for transfers between devices, body(): both = lax.all_gather(both, ('dp', 'proto'), axis=0, tiled=True)  57.5 us
    pallas_call x1, Pallas kernels, sinkhorn(): pl.pallas_call(functools.partial(sinkhorn_kernel, n_dp, n_proto, wt.shape...  41.5 us
    pallas_call x1, Pallas kernels, backward(): pl.pallas_call(functools.partial(backward_kernel, n_dp, n_own * n_proto),...  38.2 us
    pallas_call x1, Pallas kernels, scatter_rows(): pl.pallas_call(functools.partial(scatter_kernel, n_proto), out_shape=jax....  7.94 us
  transfers between devices with their start and end apart: 1, of which 1 were waited for; matrix products, arithmetic and copies ran while one was open for 0% of the time, Pallas kernels for 0%

profile of v1, /device:TPU:0, one launch (start us, length us, event | category | flops | bytes accessed | tf_op | source)
XLA Modules:
  0.0 167.8 jit_solution(10457318675990120712)
XLA Ops:
  7.2 0.0 all-gather.2.cloned.1.call-start
  7.2 0.8 fusion
  8.0 0.8 fusion.2
  8.9 0.8 fusion.1
  9.7 0.6 pad_maximum_fusion
  10.3 0.0 all-gather.2.cloned.1.call-update
  10.4 57.5 %all-gather.2.cloned.1.call-done = bf16[1024,512]{1,0:T(8,128)(2,1)} async-done(((bf16[32,512]{1,0:T(8,128)(2,1)}), bf16[1024,512]{1,0:T(8,128)(2,1)}) %all-gather.2.cloned.1.call-update) | async-done | bytes 1048592 | tf_op jit(solution)/shard_map/all_gather | solution.py:288
  67.8 2.1 %fusion.4 = (bf16[1024,256]{1,0:T(8,128)(2,1)}, bf16[256,1024]{0,1:T(8,128)(2,1)S(1)}, bf16[256,1024]{0,1:T(8,128)(2,1)S(1)}) fusion(bf16[1024,512]{1,0:T(8,128)(2,1)} %all-gather.2.cloned.1.call-done), kind=kLoop, calls=%fused_computation.13 | loop fusion | bytes 2621440 | tf_op jit(solution)/shard_map/slice | solution.py:289
  69.9 1.0 copy.9.sT_ref
  71.0 1.0 copy.8.tT_ref
  72.0 41.5 %sinkhorn.1.rows_ref = f32[8,1024]{1,0:T(8,128)} custom-call(bf16[256,1024]{1,0:T(8,128)(2,1)} %copy.8.tT_ref, bf16[256,1024]{1,0:T(8,128)(2,1)} %copy.9.sT_ref, bf16[8192,256]{1,0:T(8,128)(2,1)} %wt_ref.1, bf16[8192,256]{1,0:T(8,128)(2,1)} %ws_ref.1), custom_call_target="tpu_custom_call" | custom-call | tf_op jit(solution)/shard_map/sinkhorn/pallas_call | solution.py:159
  113.5 38.2 %backward.1 = (f32[8192,256]{1,0:T(8,128)}, f32[256,256]{1,0:T(8,128)}) custom-call(bf16[256,1024]{1,0:T(8,128)(2,1)} %copy.8.tT_ref, bf16[256,1024]{1,0:T(8,128)(2,1)} %copy.9.sT_ref, bf16[1024,256]{1,0:T(8,128)(2,1)} %get-tuple-element.6.s_ref, f32[8,1024]{1,0:T(8,128)} %sinkhorn.1.rows_ref, bf16[8192,256]{1,0:T(8,128)(2,1)} %wt_ref.1, ...), custom_call_target="tpu_custom_call" | custom-call | tf_op jit(solution)/shard_map/backward/pallas_call | solution.py:220
  151.6 7.9 %scatter_rows.1 = f32[32,256]{1,0:T(8,128)} custom-call(f32[256,256]{1,0:T(8,128)} %get-tuple-element.4.g_ref, bf16[32,256]{1,0:T(8,128)(2,1)} %s_ref.1), custom_call_target="tpu_custom_call" | custom-call | tf_op jit(solution)/shard_map/scatter_rows/pallas_call | solution.py:269
  159.6 1.4 copy.11
  (2 shorter events, 0.0 us)
Async XLA Ops:
  7.2 60.7 %all-gather.2.cloned.1.call-start = ((), (), s32[]{:S(2)}) async-start(), calls=%async_computation | async-start | bytes 1081344 | tf_op jit(solution)/shard_map/all_gather | solution.py:288
Sparse Core Ops, SparseCore 0:
  11.4 56.3 all-gather.1

commit v2 on v1

v2 whole, which is shorter than its diff:
```python
import functools
import math

import jax
import jax.numpy as jnp
from jax import lax
from jax.experimental import pallas as pl
from jax.experimental.pallas import tpu as pltpu
from jax.sharding import PartitionSpec as P

ITERS = 3
LANES = 128

teacher_temp = 0.04
student_temp = 0.1
norm_eps = 1e-06
LOG2E = math.log2(math.e)
VMEM_BYTES = 56 * 1024 * 1024

MESH = pl.DeviceIdType.MESH
f32 = jnp.float32
bf16 = jnp.bfloat16


def inv_norm(vf):
    return lax.rsqrt(jnp.sum(vf * vf, axis=-1, keepdims=True) + norm_eps)


def unit_bf16(values):
    vf = values.astype(f32)
    return (vf * inv_norm(vf)).astype(bf16)


def dot_nn(a, b):
    return jnp.dot(a, b, preferred_element_type=f32)


def fold8(x):
    return jnp.sum(x.reshape(x.shape[0] // 8, 8, x.shape[1]), axis=0)


def greet(n_dp, n_proto):
    me_d, me_p = lax.axis_index("dp"), lax.axis_index("proto")
    barrier = pltpu.get_barrier_semaphore()
    for k in range(1, n_dp):
        pl.semaphore_signal(barrier, inc=1, device_id={"dp": lax.rem(me_d + k, n_dp)}, device_id_type=MESH)
    for k in range(1, n_proto):
        pl.semaphore_signal(barrier, inc=1, device_id={"proto": lax.rem(me_p + k, n_proto)}, device_id_type=MESH)
    return barrier


def sinkhorn_kernel(
    n_dp, n_proto, n_protos, tile, small, unroll,
    t_ref, s_ref, wt_hbm, ws_hbm, out_ref, tT_ref, sT_ref, su_ref,
    e_ref, wt_ref, ws_ref, gt, gs, rxd, rxp, in_sem, sz, rz, sx, rx, sc, rc, sd, rd, sp, rp,
):
    n_rows = tT_ref.shape[1]
    own = wt_ref.shape[0]
    rb = n_rows // LANES
    nq = n_proto // 2
    me_d, me_p = lax.axis_index("dp"), lax.axis_index("proto")
    q, c = lax.div(me_p, 2), lax.rem(me_p, 2)
    off = pl.multiple_of(me_d * own, own)
    in_t = pltpu.make_async_copy(wt_hbm.at[pl.ds(off, own)], wt_ref, in_sem.at[0])
    in_s = pltpu.make_async_copy(ws_hbm.at[pl.ds(off, own)], ws_ref, in_sem.at[1])
    in_t.start()
    in_s.start()
    barrier = greet(n_dp, n_proto)
    gt[me_d, me_p] = unit_bf16(t_ref[...])
    gs[me_d, me_p] = unit_bf16(s_ref[...])
    pl.semaphore_wait(barrier, n_dp + n_proto - 2)

    def remote(ref, send, recv, to):
        return pltpu.make_async_remote_copy(
            src_ref=ref, dst_ref=ref, send_sem=send, recv_sem=recv, device_id=to, device_id_type=MESH
        )

    def along_dp(w, buf):
        return [
            remote(buf.at[me_d, me_p], sz.at[w, k], rz.at[w, k], {"dp": lax.rem(me_d + k, n_dp)})
            for k in range(1, n_dp)
        ]

    def in_plane(w, buf):
        return [
            remote(buf.at[:, me_p], sx.at[w, k], rx.at[w, k], {"proto": 2 * lax.rem(q + k, nq) + c})
            for k in range(1, nq)
        ]

    def to_core(w, buf):
        return [
            remote(buf.at[:, 2 * lax.rem(q + nq - k, nq) + c], sc.at[w, k], rc.at[w, k], {"proto": me_p + 1 - 2 * c})
            for k in range(nq)
        ]

    bufs = (gt, gs)
    dps = [along_dp(w, bufs[w]) for w in range(2)]
    planes = [in_plane(w, bufs[w]) for w in range(2)]
    cores = [to_core(w, bufs[w]) for w in range(2)]
    for w in range(2):
        for copy in dps[w]:
            copy.start()

    def spread(w):
        for copy in dps[w]:
            copy.wait_recv()
        for copy in planes[w]:
            copy.start()
        cores[w][0].start()

    def hand_on(w):
        for k in range(1, nq):
            planes[w][k - 1].wait_recv()
            cores[w][k].start()

    def arrived(w):
        for copy in cores[w]:
            copy.wait_recv()

    spread(0)
    in_t.wait()
    wt_ref[...] = unit_bf16(wt_ref[...])
    spread(1)
    hand_on(0)
    in_s.wait()
    ws_ref[...] = unit_bf16(ws_ref[...])
    arrived(0)
    tT_ref[...] = gt[...].reshape(n_rows, gt.shape[3]).T

    zero = jnp.zeros((8, n_rows), f32)

    def first(i, acc):
        at = pl.ds(pl.multiple_of(i * tile, tile), tile)
        z = dot_nn(wt_ref[at, :], tT_ref[...])
        e = jnp.exp2(z * (LOG2E / teacher_temp))
        e_ref[at, :] = e
        col = 1.0 / (n_protos * jnp.sum(e, axis=1, keepdims=True))
        return acc + fold8(e * col)

    def student(i, acc):
        at = pl.ds(pl.multiple_of(i * tile, tile), tile)
        z = dot_nn(ws_ref[at, :], sT_ref[...])
        return acc + fold8(jnp.exp2(z * (LOG2E / student_temp)))

    def put(it, acc, part):
        row = jnp.sum(acc, axis=0, keepdims=True)
        for k in range(rb):
            rxd[it, me_d, part * rb + k : part * rb + k + 1, :] = row[:, k * LANES : (k + 1) * LANES]

    def take(tot, part):
        return jnp.concatenate([tot[part * rb + k : part * rb + k + 1, :] for k in range(rb)], axis=1)

    def sends(it, ref, me, n, axis, send, recv, rows):
        copies = [
            remote(ref.at[it, me, pl.ds(0, rows)], send.at[it, k], recv.at[it, k], {axis: lax.rem(me + k, n)})
            for k in range(1, n)
        ]
        for copy in copies:
            copy.start()
        return copies

    def total_of(it, ref, n, rows):
        tot = ref[it, 0, 0:rows, :]
        for k in range(1, n):
            tot = tot + ref[it, k, 0:rows, :]
        return tot

    acc = lax.fori_loop(0, own // tile, first, zero)
    row_weight = jnp.ones((1, n_rows), f32)
    acc_s = zero
    half = own // tile // 2
    late = []
    for it in range(ITERS):
        prev = row_weight
        if it > 0:

            def again(i, acc, prev=prev):
                for j in range(unroll):
                    at = pl.ds(pl.multiple_of((i * unroll + j) * small, small), small)
                    e = e_ref[at, :]
                    col = 1.0 / (n_protos * jnp.sum(e * prev, axis=1, keepdims=True))
                    acc = acc + fold8(e * col)
                return acc

            acc = lax.fori_loop(0, own // (small * unroll), again, zero)
        last = it == ITERS - 1
        rows = 2 * rb if last else rb
        put(it, acc, 0)
        if last:
            put(it, acc_s, 1)
        copies = sends(it, rxd, me_d, n_dp, "dp", sd, rd, rows)
        late += copies
        if it == 0:
            hand_on(1)
        if it == 1:
            acc_s = lax.fori_loop(0, half, student, acc_s)
        for copy in copies:
            copy.wait_recv()
        rxp[it, me_p, 0:rows, :] = total_of(it, rxd, n_dp, rows)
        copies = sends(it, rxp, me_p, n_proto, "proto", sp, rp, rows)
        late += copies
        if it == 0:
            arrived(1)
            su_ref[...] = gs[...].reshape(n_rows, gs.shape[3])
            sT_ref[...] = su_ref[...].T
        if it == 1:
            acc_s = lax.fori_loop(half, own // tile, student, acc_s)
        for copy in copies:
            copy.wait_recv()
        tot = total_of(it, rxp, n_proto, rows)
        row_weight = 1.0 / (n_rows * take(tot, 0))
    total = take(tot, 1)
    out_ref[...] = jnp.zeros_like(out_ref)
    out_ref[0:1, :] = prev
    out_ref[1:2, :] = row_weight * (n_rows / student_temp)
    out_ref[2:3, :] = (1.0 / student_temp) / total
    for w in range(2):
        late += dps[w] + planes[w] + cores[w]
    for copy in late:
        copy.wait_send()


def sinkhorn(t, s, wt, ws, n_dp, n_proto, tile=512, small=32, unroll=8):
    mine, d = t.shape
    n_rows = mine * n_dp * n_proto
    own = wt.shape[0] // n_dp
    rb = n_rows // LANES
    nq = n_proto // 2
    sems = pltpu.SemaphoreType.DMA
    vm = pl.BlockSpec(memory_space=pltpu.VMEM)
    anym = pl.BlockSpec(memory_space=pl.ANY)
    return pl.pallas_call(
        functools.partial(sinkhorn_kernel, n_dp, n_proto, wt.shape[0] * n_proto, tile, small, unroll),
        out_shape=(
            jax.ShapeDtypeStruct((8, n_rows), f32),
            jax.ShapeDtypeStruct((d, n_rows), bf16),
            jax.ShapeDtypeStruct((d, n_rows), bf16),
            jax.ShapeDtypeStruct((n_rows, d), bf16),
        ),
        in_specs=[vm, vm, anym, anym],
        out_specs=(vm, vm, vm, vm),
        scratch_shapes=[
            pltpu.VMEM((own, n_rows), f32),
            pltpu.VMEM((own, d), bf16),
            pltpu.VMEM((own, d), bf16),
            pltpu.VMEM((n_dp, n_proto, mine, d), bf16),
            pltpu.VMEM((n_dp, n_proto, mine, d), bf16),
            pltpu.VMEM((ITERS, n_dp, 2 * rb, LANES), f32),
            pltpu.VMEM((ITERS, n_proto, 2 * rb, LANES), f32),
            sems((2,)),
            sems((2, n_dp)),
            sems((2, n_dp)),
            sems((2, nq)),
            sems((2, nq)),
            sems((2, nq)),
            sems((2, nq)),
            sems((ITERS, n_dp)),
            sems((ITERS, n_dp)),
            sems((ITERS, n_proto)),
            sems((ITERS, n_proto)),
        ],
        compiler_params=pltpu.CompilerParams(collective_id=0, has_side_effects=True, vmem_limit_bytes=VMEM_BYTES),
        name="sinkhorn",
    )(t, s, wt, ws)


def backward_kernel(
    n_dp, n_protos, sub, tT_ref, sT_ref, s_ref, rows_ref, wt_ref, ws_ref, out_ref, grow_ref, dz_ref, wsh_ref
):
    n_rows = tT_ref.shape[1]
    mine = n_rows // n_dp
    factor = n_protos / n_rows
    a_prev, a_last, p_last = rows_ref[0:1, :], rows_ref[1:2, :], rows_ref[2:3, :]
    for j in range(wt_ref.shape[0] // sub):
        at = slice(j * sub, (j + 1) * sub)
        zt = dot_nn(unit_bf16(wt_ref[at, :]), tT_ref[...])
        wsf = ws_ref[at, :].astype(f32)
        ws_inv = inv_norm(wsf)
        ws_unit = wsf * ws_inv
        ws_half = ws_unit.astype(bf16)
        wsh_ref[at, :] = ws_half
        zs = dot_nn(ws_half, sT_ref[...])
        e = jnp.exp2(zt * (LOG2E / teacher_temp))
        col = 1.0 / (n_protos * jnp.sum(e * a_prev, axis=1, keepdims=True))
        probs = jnp.exp2(zs * (LOG2E / student_temp)) * p_last
        dz = (probs - (e * a_last) * col).astype(bf16)
        dz_ref[at, :] = dz
        g = dot_nn(dz, s_ref[...])
        proj = jnp.sum(g * ws_unit, axis=1, keepdims=True)
        out_ref[at, :] = (g - proj * ws_unit) * (factor * ws_inv)
    own_rows = pl.ds(pl.multiple_of(lax.axis_index("dp") * mine, mine), mine)
    part = lax.dot_general(
        dz_ref[:, own_rows], wsh_ref[...], (((0,), (0,)), ((), ())), preferred_element_type=f32
    )

    @pl.when(pl.program_id(0) == 0)
    def _():
        grow_ref[...] = jnp.zeros_like(grow_ref)

    grow_ref[...] += part


def backward(tT, sT, s, rows, wt, ws, n_dp, n_proto, tile=None, sub=None):
    d, n_rows = tT.shape
    n_own = wt.shape[0]
    tile = tile or max(256, (1 << 20) // n_rows)
    sub = sub or 256
    const = lambda shape: pl.BlockSpec(shape, lambda i: (0, 0))
    tiled = pl.BlockSpec((tile, d), lambda i: (i, 0))
    mine = n_rows // n_dp
    return pl.pallas_call(
        functools.partial(backward_kernel, n_dp, n_own * n_proto, sub),
        grid=(n_own // tile,),
        out_shape=(jax.ShapeDtypeStruct((n_own, d), f32), jax.ShapeDtypeStruct((mine, d), f32)),
        in_specs=[const((d, n_rows)), const((d, n_rows)), const((n_rows, d)), const((8, n_rows)), tiled, tiled],
        out_specs=(tiled, const((mine, d))),
        scratch_shapes=[pltpu.VMEM((tile, n_rows), bf16), pltpu.VMEM((tile, d), bf16)],
        compiler_params=pltpu.CompilerParams(vmem_limit_bytes=VMEM_BYTES),
        name="backward",
    )(tT, sT, s, rows, wt, ws)


def scatter_kernel(n, g_ref, s_ref, out_ref, rx, send, recv):
    me = lax.axis_index("proto")
    own = out_ref.shape[0]
    barrier = pltpu.get_barrier_semaphore()
    for k in range(1, n):
        pl.semaphore_signal(barrier, inc=1, device_id={"proto": lax.rem(me + k, n)}, device_id_type=MESH)
    pl.semaphore_wait(barrier, n - 1)
    copies = []
    for k in range(1, n):
        to = lax.rem(me + k, n)
        copies.append(
            pltpu.make_async_remote_copy(
                src_ref=g_ref.at[pl.ds(pl.multiple_of(to * own, own), own)],
                dst_ref=rx.at[me],
                send_sem=send.at[k],
                recv_sem=recv.at[k],
                device_id={"proto": to},
                device_id_type=MESH,
            )
        )
    for c in copies:
        c.start()
    rx[me] = g_ref[pl.ds(pl.multiple_of(me * own, own), own), :]
    sf = s_ref[...].astype(f32)
    inv = inv_norm(sf)
    unit = sf * inv
    for c in copies:
        c.wait()
    g = rx[0]
    for k in range(1, n):
        g = g + rx[k]
    out_ref[...] = (g - jnp.sum(g * unit, axis=1, keepdims=True) * unit) * inv


def scatter_rows(grow, student_rows, n_proto):
    vm = pl.BlockSpec(memory_space=pltpu.VMEM)
    own, d = student_rows.shape
    return pl.pallas_call(
        functools.partial(scatter_kernel, n_proto),
        out_shape=jax.ShapeDtypeStruct((own, d), f32),
        in_specs=[vm, vm],
        out_specs=vm,
        scratch_shapes=[
            pltpu.VMEM((n_proto, own, d), f32),
            pltpu.SemaphoreType.DMA((n_proto,)),
            pltpu.SemaphoreType.DMA((n_proto,)),
        ],
        compiler_params=pltpu.CompilerParams(collective_id=1, has_side_effects=True),
        name="scatter_rows",
    )(grow, student_rows)


def body(teacher_rows, student_rows, teacher_protos, student_protos):
    n_dp, n_proto = lax.axis_size("dp"), lax.axis_size("proto")
    stats, tT, sT, s_unit = sinkhorn(teacher_rows, student_rows, teacher_protos, student_protos, n_dp, n_proto)
    proto_grads, grow = backward(tT, sT, s_unit, stats, teacher_protos, student_protos, n_dp, n_proto)
    row_grads = scatter_rows(grow, student_rows, n_proto)
    return (row_grads, proto_grads)


def solution(mesh):
    rows = P(("dp", "proto"), None)
    protos = P("proto", None)
    return jax.shard_map(
        body,
        mesh=mesh,
        in_specs=(rows, rows, protos, protos),
        out_specs=(rows, protos),
        check_vma=False,
    )
```

time: 168 us -> 79.7 us (0.47)
  waiting for transfers between devices: 57.5 us -> 0 us
  between operations: 14.1 us -> 0.65 us
  Pallas kernels: 87.6 us -> 77.3 us
  local copies, waits for them, and re-layouts: 5.5 us -> 1.38 us
  other arithmetic: 3.12 us -> 0 us
    all_gather x1 -> x0, waiting for transfers between devices: 57.5 us -> none  [body(): both = lax.all_gather(both, ('dp', 'proto'), axis=0, tiled=True)]
    pallas_call x1, Pallas kernels: 38.2 us -> 25.8 us  [backward(): pl.pallas_call(functools.partial(backward_kernel, n_dp, n_own * n_proto,...]
    slice x1 -> x0, local copies, waits for them, and re-layouts: 2.12 us -> none  [body(): s_unit = both[:, d:]]
    transpose x2 -> x0, local copies, waits for them, and re-layouts: 2.01 us -> none  [body(): tT, sT = (both[:, :d].T, s_unit.T)]
    pallas_call x1, Pallas kernels: 41.5 us -> 43.5 us  [sinkhorn(): pl.pallas_call(functools.partial(sinkhorn_kernel, n_dp, n_proto, wt.shape...]
  transfers between devices with their start and end apart: 1 -> 0, of which waited for: 1 -> 0; matrix products, arithmetic and copies ran while one was open for 0% -> 0% of each run, Pallas kernels for 0% -> 0%
where the time goes in v2:
time: 79.7 us; the launch traced here: 79.3 us
  Pallas kernels  77.3 us (97%)
  local copies, waits for them, and re-layouts  1.38 us (2%)
    pallas_call x1, Pallas kernels, sinkhorn(): pl.pallas_call(functools.partial(sinkhorn_kernel, n_dp, n_proto, wt.shape...  43.5 us
    pallas_call x1, Pallas kernels, backward(): pl.pallas_call(functools.partial(backward_kernel, n_dp, n_own * n_proto,...  25.8 us
    pallas_call x1, Pallas kernels, scatter_rows(): pl.pallas_call(functools.partial(scatter_kernel, n_proto), out_shape=jax....  8.01 us

profile of v2, /device:TPU:0, one launch (start us, length us, event | category | flops | bytes accessed | tf_op | source)
XLA Modules:
  0.0 79.3 jit_solution(9436143159810643955)
XLA Ops:
  0.6 43.5 %sinkhorn.1 = (f32[8,1024]{1,0:T(8,128)}, bf16[256,1024]{1,0:T(8,128)(2,1)}, bf16[256,1024]{1,0:T(8,128)(2,1)}, bf16[1024,256]{1,0:T(8,128)(2,1)}) custom-call(bf16[32,256]{1,0:T(8,128)(2,1)} %t_ref.1, bf16[32,256]{1,0:T(8,128)(2,1)} %s_ref.3, bf16[8192,256]{1,0:T(8,128)(2,1)} %wt_ref.1, bf16[8192,256]{1,0:T(8,128)(2,1)} %ws_ref.1), custom_call_target="tpu_custom_call" | custom-call | tf_op jit(solution)/shard_map/sinkhorn/pallas_call | solution.py:232
  44.1 25.8 %backward.1 = (f32[8192,256]{1,0:T(8,128)}, f32[256,256]{1,0:T(8,128)}) custom-call(bf16[256,1024]{1,0:T(8,128)(2,1)} %get-tuple-element.8.tT_ref, bf16[256,1024]{1,0:T(8,128)(2,1)} %get-tuple-element.9.sT_ref, bf16[1024,256]{1,0:T(8,128)(2,1)} %get-tuple-element.10.s_ref, f32[8,1024]{1,0:T(8,128)} %get-tuple-element.11.rows_ref, bf16[8192,256]{1,0:T(8,128)(2,1)} %wt_ref.1, ...), custom_call_target="tpu_custom_call" | custom-call | tf_op jit(solution)/shard_map/backward/pallas_call | solution.py:311
  69.9 8.0 %scatter_rows.1 = f32[32,256]{1,0:T(8,128)} custom-call(f32[256,256]{1,0:T(8,128)} %get-tuple-element.12.g_ref, bf16[32,256]{1,0:T(8,128)(2,1)} %s_ref.3), custom_call_target="tpu_custom_call" | custom-call | tf_op jit(solution)/shard_map/scatter_rows/pallas_call | solution.py:360
  78.0 1.4 %copy.7 = f32[32,256]{1,0:T(8,128)} copy(f32[32,256]{1,0:T(8,128)} %scatter_rows.1) | data formatting | bytes 65536

commit v3 on v2

--- a/solution.py
+++ b/solution.py
@@ -83,45 +83,62 @@
 
     def in_plane(w, buf):
         return [
-            remote(buf.at[:, me_p], sx.at[w, k], rx.at[w, k], {"proto": 2 * lax.rem(q + k, nq) + c})
-            for k in range(1, nq)
+            [
+                remote(
+                    buf.at[lax.rem(me_d + n_dp - d, n_dp), me_p],
+                    sx.at[w, d, k], rx.at[w, d, k], {"proto": 2 * lax.rem(q + k, nq) + c},
+                )
+                for k in range(1, nq)
+            ]
+            for d in range(n_dp)
         ]
 
     def to_core(w, buf):
         return [
-            remote(buf.at[:, 2 * lax.rem(q + nq - k, nq) + c], sc.at[w, k], rc.at[w, k], {"proto": me_p + 1 - 2 * c})
-            for k in range(nq)
+            [
+                remote(
+                    buf.at[lax.rem(me_d + n_dp - d, n_dp), 2 * lax.rem(q + nq - k, nq) + c],
+                    sc.at[w, d, k], rc.at[w, d, k], {"proto": me_p + 1 - 2 * c},
+                )
+                for k in range(nq)
+            ]
+            for d in range(n_dp)
         ]
 
     bufs = (gt, gs)
     dps = [along_dp(w, bufs[w]) for w in range(2)]
     planes = [in_plane(w, bufs[w]) for w in range(2)]
     cores = [to_core(w, bufs[w]) for w in range(2)]
-    for w in range(2):
-        for copy in dps[w]:
-            copy.start()
-
-    def spread(w):
-        for copy in dps[w]:
-            copy.wait_recv()
-        for copy in planes[w]:
-            copy.start()
-        cores[w][0].start()
+    for copy in dps[0]:
+        copy.start()
+
+    def spread(w, ds):
+        for d in ds:
+            if d:
+                dps[w][d - 1].wait_recv()
+            for copy in planes[w][d]:
+                copy.start()
+            cores[w][d][0].start()
 
     def hand_on(w):
-        for k in range(1, nq):
-            planes[w][k - 1].wait_recv()
-            cores[w][k].start()
+        for d in range(n_dp):
+            for k in range(1, nq):
+                planes[w][d][k - 1].wait_recv()
+                cores[w][d][k].start()
 
     def arrived(w):
-        for copy in cores[w]:
-            copy.wait_recv()
-
-    spread(0)
+        for row in cores[w]:
+            for copy in row:
+                copy.wait_recv()
+
+    spread(0, [0])
+    for copy in dps[1]:
+        copy.start()
+    spread(0, range(1, n_dp))
     in_t.wait()
     wt_ref[...] = unit_bf16(wt_ref[...])
-    spread(1)
     hand_on(0)
+    spread(1, range(n_dp))
     in_s.wait()
     ws_ref[...] = unit_bf16(ws_ref[...])
     arrived(0)
@@ -215,7 +232,7 @@
     out_ref[1:2, :] = row_weight * (n_rows / student_temp)
     out_ref[2:3, :] = (1.0 / student_temp) / total
     for w in range(2):
-        late += dps[w] + planes[w] + cores[w]
+        late += dps[w] + sum(planes[w], []) + sum(cores[w], [])
     for copy in late:
         copy.wait_send()
 
@@ -250,10 +267,10 @@
             sems((2,)),
             sems((2, n_dp)),
             sems((2, n_dp)),
-            sems((2, nq)),
-            sems((2, nq)),
-            sems((2, nq)),
-            sems((2, nq)),
+            sems((2, n_dp, nq)),
+            sems((2, n_dp, nq)),
+            sems((2, n_dp, nq)),
+            sems((2, n_dp, nq)),
             sems((ITERS, n_dp)),
             sems((ITERS, n_dp)),
             sems((ITERS, n_proto)),

time: 79.7 us -> 78.9 us (0.990)
  no operation moved by 1% of the time
where the time goes in v3:
time: 78.9 us; the launch traced here: 78.6 us
  Pallas kernels  76.6 us (97%)
  local copies, waits for them, and re-layouts  1.38 us (2%)
    pallas_call x1, Pallas kernels, sinkhorn(): pl.pallas_call(functools.partial(sinkhorn_kernel, n_dp, n_proto, wt.shape...  42.8 us
    pallas_call x1, Pallas kernels, backward(): pl.pallas_call(functools.partial(backward_kernel, n_dp, n_own * n_proto,...  25.8 us
    pallas_call x1, Pallas kernels, scatter_rows(): pl.pallas_call(functools.partial(scatter_kernel, n_proto), out_shape=jax....  7.93 us

profile of v3, /device:TPU:0, one launch (start us, length us, event | category | flops | bytes accessed | tf_op | source)
XLA Modules:
  0.0 78.6 jit_solution(12768317463248760605)
XLA Ops:
  0.6 42.8 %sinkhorn.1 = (f32[8,1024]{1,0:T(8,128)}, bf16[256,1024]{1,0:T(8,128)(2,1)}, bf16[256,1024]{1,0:T(8,128)(2,1)}, bf16[1024,256]{1,0:T(8,128)(2,1)}) custom-call(bf16[32,256]{1,0:T(8,128)(2,1)} %t_ref.1, bf16[32,256]{1,0:T(8,128)(2,1)} %s_ref.3, bf16[8192,256]{1,0:T(8,128)(2,1)} %wt_ref.1, bf16[8192,256]{1,0:T(8,128)(2,1)} %ws_ref.1), custom_call_target="tpu_custom_call" | custom-call | tf_op jit(solution)/shard_map/sinkhorn/pallas_call | solution.py:249
  43.5 25.8 %backward.1 = (f32[8192,256]{1,0:T(8,128)}, f32[256,256]{1,0:T(8,128)}) custom-call(bf16[256,1024]{1,0:T(8,128)(2,1)} %get-tuple-element.8.tT_ref, bf16[256,1024]{1,0:T(8,128)(2,1)} %get-tuple-element.9.sT_ref, bf16[1024,256]{1,0:T(8,128)(2,1)} %get-tuple-element.10.s_ref, f32[8,1024]{1,0:T(8,128)} %get-tuple-element.11.rows_ref, bf16[8192,256]{1,0:T(8,128)(2,1)} %wt_ref.1, ...), custom_call_target="tpu_custom_call" | custom-call | tf_op jit(solution)/shard_map/backward/pallas_call | solution.py:328
  69.3 7.9 %scatter_rows.1 = f32[32,256]{1,0:T(8,128)} custom-call(f32[256,256]{1,0:T(8,128)} %get-tuple-element.12.g_ref, bf16[32,256]{1,0:T(8,128)(2,1)} %s_ref.3), custom_call_target="tpu_custom_call" | custom-call | tf_op jit(solution)/shard_map/scatter_rows/pallas_call | solution.py:377
  77.2 1.4 %copy.7 = f32[32,256]{1,0:T(8,128)} copy(f32[32,256]{1,0:T(8,128)} %scatter_rows.1) | data formatting | bytes 65536
